TPU v7x, 32 devices: a whole 2x2x4 slice. The times are simulated.
32 devices in a mesh: groups: 2 (over x), rows: 8 (over z, y), proj: 2 (over core).
Axes of the slice: x: 2, y: 2, z: 4, core: 2. Of those that a mesh axis runs over, the one named last changes fastest.
Arguments:
- train_rows: float32 [5120, 4, 8192], P(('groups', 'rows'), None, 'proj'), parts along dimension 0, may hold values from -6 to 6
- weights: float32 [5120, 4], P(('groups', 'rows', 'proj')), parts along dimension 0, may hold values from 0.1 to 1
- ckpt_index: int32 [320, 4], P(('groups', 'rows')), parts along dimension 0, may hold values from 0 to 3, each once within a row
- queries: float32 [512, 4, 8192], P(('groups', 'rows'), None, 'proj'), parts along dimension 0, may hold values from -0.125 to 0.125
Outputs:
- scores: float32 [5120, 256], P(('groups', 'rows'), 'proj'), parts along dimension 0
There are 2 independent parts, one for each index of `groups`. A program takes and returns all parts, laid end to end along the dimension named above; each array names one. Nothing has to cross between parts.
Inputs may be any that keep to these rules, and one draw needn't show every extreme that they name: Each row of ckpt_index names every checkpoint once.
All inputs are finite; a program needn't handle non-finite values.
Results may differ from a plain program's by a relative error of at most 0.000073.
Values sent between devices are 32-bit elements; how exact they have to be, the bound alone decides.
A program may use at most 192 MiB of HBM per device.

v0:
```python
import jax
import jax.numpy as jnp
from jax import lax
from jax.sharding import PartitionSpec as P


def reorder(train_block, weight_block, slot_ckpt):
    ckpt_count = train_block.shape[1]
    onehot = (
        slot_ckpt[:, :, None] == jnp.arange(ckpt_count, dtype=jnp.int32)[None, None, :]
    ).astype(jnp.float32)
    weighted = weight_block[:, :, None] * train_block
    by_ckpt = jnp.einsum("isc,isk->ick", onehot, weighted, precision=lax.Precision.HIGHEST)
    return by_ckpt.reshape(train_block.shape[0], ckpt_count * train_block.shape[2])


def score_fold(stacked, block_rows):
    flat_block = block_rows.reshape(block_rows.shape[0], block_rows.shape[1] * block_rows.shape[2])
    partial_scores = lax.dot_general(
        stacked,
        flat_block,
        (((1,), (1,)), ((), ())),
        precision=lax.Precision.HIGHEST,
        preferred_element_type=jnp.float32,
    )
    return partial_scores


def on_device(train_rows, weights, ckpt_index, queries):
    rows_here = train_rows.shape[0]
    ckpt_count = train_rows.shape[1]
    slab_rows = rows_here // ckpt_index.shape[0]
    slot_ckpt = jnp.repeat(ckpt_index, slab_rows, axis=0)
    full_weights = lax.all_gather(weights, "proj", axis=0, tiled=True)
    stacked = reorder(train_rows, full_weights, slot_ckpt)
    totals = score_fold(stacked, lax.all_gather(queries, "rows", axis=0, tiled=True))
    scores = lax.psum_scatter(totals, "proj", scatter_dimension=1, tiled=True)
    return scores * (1.0 / ckpt_count)


def solution(mesh):
    placed = (
        P(("groups", "rows"), None, "proj"),
        P(("groups", "rows", "proj"), None),
        P(("groups", "rows"), None),
        P(("groups", "rows"), None, "proj"),
    )
    return jax.shard_map(
        on_device,
        mesh=mesh,
        in_specs=placed,
        out_specs=P(("groups", "rows"), "proj"),
        check_vma=False,
    )
```

profile of v0, /device:TPU:0, one launch (start us, length us, event | category | flops | bytes accessed | tf_op | source)
XLA Modules:
  0.0 289.7 jit_solution(1722394300916280541)
XLA Ops:
  6.5 0.0 all-gather.3.cloned.1.call-start
  6.5 4.1 %copy.14 = f32[32,4,4096]{2,0,1:T(8,128)} copy(f32[32,4,4096]{2,1,0:T(4,128)} %param.7) | data formatting | bytes 4194304 | tf_op args[3]
  10.7 0.0 all-gather.3.cloned.1.call-update
  10.7 0.0 reduce-scatter.2.cloned.1.call-start
  10.7 0.8 copy.11
  11.5 2.1 all-gather
  13.6 0.1 copy.16
  13.7 27.1 %fusion.2 = f32[320,4,4096]{2,1,0:T(4,128)} fusion(f32[320,4,4096]{2,1,0:T(4,128)} %param.4, f32[320,4]{1,0:T(8,128)S(1)} %bitcast.6, s32[320,4]{1,0:T(8,128)S(1)} %bitcast.7), kind=kOutput, calls=%fused_computation.2 | convolution fusion | flops 256906240 | bytes 41953280 | tf_op jit(solution)/shard_map/isc,isk->ick/dot_general | solution.py:13
  40.9 200.3 %all-gather.3.cloned.1.call-done = f32[256,4,4096]{2,0,1:T(8,128)} async-done(((f32[32,4,4096]{2,0,1:T(8,128)}), f32[256,4,4096]{2,0,1:T(8,128)}) %all-gather.3.cloned.1.call-update) | async-done | bytes 16777232 | tf_op jit(solution)/shard_map/all_gather | solution.py:36
  241.1 34.0 %fusion.5 = f32[320,256]{1,0:T(8,128)} fusion(f32[256,4,4096]{2,0,1:T(8,128)} %all-gather.3.cloned.1.call-done, f32[320,4,4096]{2,1,0:T(4,128)} %fusion.2), kind=kOutput, calls=%fused_computation.5 | convolution fusion | flops 16106127360 | bytes 38076416 | tf_op jit(solution)/shard_map/dot_general | solution.py:19
  275.2 0.0 reduce-scatter.2.cloned.1.call-update
  275.2 6.1 %reduce-scatter.2.cloned.1.call-done = f32[320,128]{1,0:T(8,128)} async-done(((f32[320,256]{1,0:T(8,128)}), f32[320,128]{1,0:T(8,128)}) %reduce-scatter.2.cloned.1.call-update) | async-done | bytes 163856 | tf_op jit(solution)/shard_map/reduce_scatter | solution.py:37
  281.3 1.6 broadcast_multiply_fusion
  (1 shorter events, 0.0 us)
Async XLA Ops:
  6.5 234.6 %all-gather.3.cloned.1.call-start = ((), (), s32[]{:S(2)}) async-start(), calls=%async_computation.1 | async-start | bytes 18874368 | tf_op jit(solution)/shard_map/all_gather | solution.py:36
  10.7 270.6 %reduce-scatter.2.cloned.1.call-start = ((), (), s32[]{:S(2)}) async-start(), calls=%async_computation.2 | async-start | bytes 491520 | tf_op jit(solution)/shard_map/reduce_scatter | solution.py:37
Sparse Core Ops, SparseCore 0:
  10.8 230.2 all-gather.2
  275.3 5.9 reduce-scatter.1
where the time goes:
time: 290 us
  waiting for transfers between devices  206 us (71%)
  matrix products  61.2 us (21%)
  between operations  13.4 us (5%)
  local copies, waits for them, and re-layouts  5.05 us (2%)
    all_gather x1, waiting for transfers between devices, on_device(): lax.all_gather(queries, 'rows', axis=0, tiled=True)  200 us
    dot_general x1, matrix products, score_fold(): lax.dot_general(stacked, flat_block, (((1,), (1,)), ((), ())), precision=...  34 us
    dot_general x1, matrix products, reorder(): jnp.einsum('isc,isk->ick', onehot, weighted, precision=lax.Precision.HIGH...  27.1 us
    reduce_scatter x1, waiting for transfers between devices, on_device(): scores = lax.psum_scatter(totals, 'proj', scatter_dimension=1, tiled=True)  6.08 us
  transfers between devices with their start and end apart: 2, of which 2 were waited for; matrix products, arithmetic and copies ran while one was open for 10% of the time, Pallas kernels for 0%

commit v1 on v0

v1 whole, which is shorter than its diff:
```python
import functools

import jax
import jax.numpy as jnp
from jax import lax
from jax.experimental import pallas as pl
from jax.experimental.pallas import tpu as pltpu
from jax.sharding import PartitionSpec as P

MESH = pl.DeviceIdType.MESH
PIECES = 8
LAG = 2


def kernel(n, train, weights, ckpt, queries, gat, mine, theirs,
           th, tl, tbuf, qtile, acc, wfull, pout,
           recv, send, fetch, tsem, wsem, psem):
    line = n // 2
    main = PIECES - 1
    per_step = main + 2
    y_slots = PIECES + (line - 1) * main
    z_slots = (line - 1) * per_step
    slots = max(y_slots, z_slots)
    rows, ckpts, depth = train.shape
    count = queries.shape[0]
    width = depth // PIECES
    lanes = count * ckpts
    half_cols = mine.shape[1]

    me = lax.axis_index("rows")
    core = lax.axis_index("proj")
    z, y = lax.div(me, 2), lax.rem(me, 2)
    across = {"rows": z * 2 + (1 - y)}
    above = {"rows": me + 2}
    below = {"rows": me - 2}
    partner = {"proj": 1 - core}

    def part(ref, piece):
        return ref.at[:, :, pl.ds(pl.multiple_of(piece * width, width), width)]

    def by_arrival(k):
        m = jnp.minimum(z, line - 1 - z)
        far = k - m + 1
        near = jnp.where(lax.rem(k, 2) == 0, z - lax.div(k, 2) - 1, z + lax.div(k, 2) + 1)
        rest = jnp.where(2 * z < line - 1, z + far, z - far)
        return jnp.where(k < 2 * m, near, rest)

    def y_item(t, col):
        first = t < PIECES
        v = jnp.maximum(t - PIECES, 0)
        other = by_arrival(lax.div(v, main))
        zb = jnp.where(first, z, other)
        piece = jnp.where(first, lax.rem(t + PIECES - 1, PIECES), lax.rem(v, main))
        return zb * 2 + col, piece

    def z_item(t, start, sign):
        s, i = lax.div(t, per_step), lax.rem(t, per_step)
        zb = start + sign * s
        col = jnp.where(i == per_step - 1, 1 - y, y)
        piece = jnp.minimum(i, PIECES - 1)
        ok = (t < z_slots) & (zb >= 0) & (zb < line)
        own = (s == 0) & (i < PIECES)
        return jnp.clip(zb, 0, line - 1) * 2 + col, piece, ok, own

    def copy_to(src, block, piece, lane, u, device):
        return pltpu.make_async_remote_copy(
            src_ref=part(src, piece),
            dst_ref=part(gat.at[block], piece),
            send_sem=send.at[lane, lax.rem(u, 8)],
            recv_sem=recv.at[block, piece],
            device_id=device,
            device_id_type=MESH,
        )

    def sends(u):
        block, piece = y_item(u, y)

        @pl.when(u < PIECES)
        def _():
            copy_to(queries, block, piece, 0, u, across).start()

        @pl.when((u >= PIECES) & (u < y_slots))
        def _():
            copy_to(gat.at[block], block, piece, 0, u, across).start()

        for lane, device, sign, there in ((1, above, -1, z < line - 1), (2, below, 1, z > 0)):
            block, piece, ok, own = z_item(u, z, sign)

            @pl.when(there & ok & own)
            def _():
                copy_to(queries, block, piece, lane, u, device).start()

            @pl.when(there & ok & jnp.logical_not(own))
            def _():
                copy_to(gat.at[block], block, piece, lane, u, device).start()

    def wait_sends(u):
        @pl.when((u >= 0) & (u < y_slots))
        def _():
            copy_to(queries, me, 0, 0, u, across).wait_send()

        for lane, device, sign, there in ((1, above, -1, z < line - 1), (2, below, 1, z > 0)):
            ok = z_item(jnp.maximum(u, 0), z, sign)[2]

            @pl.when(there & ok & (u >= 0))
            def _():
                copy_to(queries, me, 0, lane, u, device).wait_send()

    def arrivals(t):
        block, piece = y_item(t, 1 - y)
        found = [(block, piece, t < y_slots)]
        for start, sign in ((z - 1, -1), (z + 1, 1)):
            block, piece, ok, _ = z_item(t, start, sign)
            found.append((block, piece, ok))
        found.append((me, lax.rem(t + PIECES - 1, PIECES), t < PIECES))
        return found

    def fetch_copy(src, piece, t, j):
        return pltpu.make_async_copy(part(src, piece), qtile.at[lax.rem(t, 2), j], fetch.at[lax.rem(t, 2), j])

    def take(t):
        for j, (block, piece, ok) in enumerate(arrivals(t)):
            @pl.when(ok)
            def _():
                if j < 3:
                    copy_to(queries, block, piece, 0, 0, across).wait_recv()
                    fetch_copy(gat.at[block], piece, t, j).start()
                else:
                    fetch_copy(queries, piece, t, j).start()

    def multiply(t):
        found = arrivals(t)

        def one(j, carry):
            def pick(values):
                return jnp.where(j == 0, values[0], jnp.where(j == 1, values[1], jnp.where(j == 2, values[2], values[3])))
            block = pick([f[0] for f in found])
            piece = pick([f[1] for f in found])
            ok = pick([f[2].astype(jnp.int32) for f in found])

            @pl.when(ok == 1)
            def _():
                fetch_copy(queries, 0, t, j).wait()
                q = qtile[lax.rem(t, 2), j].reshape(lanes, width)
                hi = q.astype(jnp.bfloat16)
                lo = (q - hi.astype(jnp.float32)).astype(jnp.bfloat16)
                ds = pl.ds(pl.multiple_of(piece * width, width), width)
                dims = (((1,), (1,)), ((), ()))
                both = jnp.concatenate([hi, lo], axis=0)
                r = lax.dot_general(th[:, ds], both, dims, preferred_element_type=jnp.float32)
                r2 = lax.dot_general(tl[:, ds], hi, dims, preferred_element_type=jnp.float32)
                acc[block] += r[:, :lanes] + r[:, lanes:] + r2
            return carry

        lax.fori_loop(0, 4, one, 0)

    def t_copy(u):
        return pltpu.make_async_copy(
            part(train, lax.rem(u + PIECES - 1, PIECES)), tbuf.at[lax.rem(u, 2)], tsem.at[lax.rem(u, 2)])

    def split(u):
        @pl.when(u + 1 < PIECES)
        def _():
            t_copy(u + 1).start()
        t_copy(u).wait()
        ds = pl.ds(pl.multiple_of(lax.rem(u + PIECES - 1, PIECES) * width, width), width)

        def some(r, carry):
            x = tbuf[lax.rem(u, 2), pl.ds(r * 16, 16)].reshape(16 * ckpts, width)
            hi = x.astype(jnp.bfloat16)
            out = pl.ds(pl.multiple_of(r * (16 * ckpts), 16 * ckpts), 16 * ckpts)
            th[out, ds] = hi
            tl[out, ds] = (x - hi.astype(jnp.float32)).astype(jnp.bfloat16)
            return carry

        lax.fori_loop(0, rows // 16, some, 0)

    t_copy(0).start()
    barrier = pltpu.get_barrier_semaphore()
    for device in (across, partner):
        pl.semaphore_signal(barrier, inc=1, device_id=device, device_id_type=MESH)

    @pl.when(z < line - 1)
    def _():
        pl.semaphore_signal(barrier, inc=1, device_id=above, device_id_type=MESH)

    @pl.when(z > 0)
    def _():
        pl.semaphore_signal(barrier, inc=1, device_id=below, device_id_type=MESH)

    pl.semaphore_wait(barrier, 2 + (z < line - 1).astype(jnp.int32) + (z > 0).astype(jnp.int32))

    here = weights.shape[0]
    w_copy = pltpu.make_async_remote_copy(
        src_ref=weights, dst_ref=wfull.at[core], send_sem=wsem.at[0], recv_sem=wsem.at[1],
        device_id=partner, device_id_type=MESH)

    def clear(b, carry):
        acc[b] = jnp.zeros(acc.shape[1:], jnp.float32)
        return carry

    def step(u, carry):
        @pl.when(u < slots)
        def _():
            sends(u)

        @pl.when(u == 0)
        def _():
            w_copy.start()
            wfull[core] = weights[...]
            lax.fori_loop(0, n, clear, 0)

        @pl.when((u >= LAG) & (u < slots + LAG))
        def _():
            take(u - LAG)

        @pl.when(u < PIECES)
        def _():
            split(u)

        @pl.when(u >= LAG + 1)
        def _():
            multiply(u - LAG - 1)

        wait_sends(u - 4)
        return carry

    last = slots + LAG + 1
    lax.fori_loop(0, last, step, 0)
    for u in range(last - 4, slots):
        wait_sends(u)
    w_copy.wait()

    w = jnp.concatenate([wfull[0], wfull[1]], axis=0)
    held = ckpt[...]
    of_lane = lax.broadcasted_iota(jnp.int32, (rows, lanes), 1) % ckpts
    coef = [jnp.where(held[:, s:s + 1] == of_lane, w[:, s:s + 1], 0.0) for s in range(ckpts)]

    def finish(half):
        def one(b, total):
            block = half * (n // 2) + b
            a = acc.at[block]
            mixed = coef[0] * a[pl.ds(0, rows, stride=ckpts), :]
            for s in range(1, ckpts):
                mixed += coef[s] * a[pl.ds(s, rows, stride=ckpts), :]
            lane = lax.broadcasted_iota(jnp.int32, (lanes, half_cols), 0)
            col = lax.broadcasted_iota(jnp.int32, (lanes, half_cols), 1)
            place = jnp.where(col - b * count == lane // ckpts, 1.0, 0.0).astype(jnp.float32)
            return total + lax.dot_general(mixed, place, (((1,), (0,)), ((), ())),
                                           precision=lax.Precision.HIGHEST,
                                           preferred_element_type=jnp.float32)
        return lax.fori_loop(0, n // 2, one, jnp.zeros((rows, half_cols), jnp.float32))

    pout[...] = finish(1 - core)
    back = pltpu.make_async_remote_copy(
        src_ref=pout, dst_ref=theirs, send_sem=psem.at[0], recv_sem=psem.at[1],
        device_id=partner, device_id_type=MESH)
    back.start()
    mine[...] = finish(core)
    back.wait()


def on_device(n, train_rows, weights, ckpt_index, queries):
    rows, ckpts, depth = train_rows.shape
    count = queries.shape[0]
    lanes = count * ckpts
    width = depth // PIECES
    half_cols = n * count // 2
    held = jnp.repeat(ckpt_index, rows // ckpt_index.shape[0], axis=0)
    anyspec = pl.BlockSpec(memory_space=pl.ANY)
    vmem = pl.BlockSpec(memory_space=pltpu.VMEM)
    part = jax.ShapeDtypeStruct((rows, half_cols), jnp.float32)
    _, mine, theirs = pl.pallas_call(
        functools.partial(kernel, n),
        out_shape=(jax.ShapeDtypeStruct((n,) + queries.shape, jnp.float32), part, part),
        in_specs=[anyspec, vmem, vmem, anyspec],
        out_specs=(anyspec, vmem, vmem),
        scratch_shapes=[
            pltpu.VMEM((rows * ckpts, depth), jnp.bfloat16),
            pltpu.VMEM((rows * ckpts, depth), jnp.bfloat16),
            pltpu.VMEM((2, rows, ckpts, width), jnp.float32),
            pltpu.VMEM((2, 4, count, ckpts, width), jnp.float32),
            pltpu.VMEM((n, rows * ckpts, lanes), jnp.float32),
            pltpu.VMEM((2, rows // 2, ckpts), jnp.float32),
            pltpu.VMEM((rows, half_cols), jnp.float32),
            pltpu.SemaphoreType.DMA((n, PIECES)),
            pltpu.SemaphoreType.DMA((3, 8)),
            pltpu.SemaphoreType.DMA((2, 4)),
            pltpu.SemaphoreType.DMA((2,)),
            pltpu.SemaphoreType.DMA((2,)),
            pltpu.SemaphoreType.DMA((2,)),
        ],
        compiler_params=pltpu.CompilerParams(
            collective_id=0, has_side_effects=True, vmem_limit_bytes=60 * 1024 * 1024),
        cost_estimate=pl.CostEstimate(
            flops=6 * rows * ckpts * depth * lanes * n, bytes_accessed=4 * rows * ckpts * depth, transcendentals=0),
    )(train_rows, weights, held, queries)
    return (mine + theirs) * (1.0 / ckpts)


def solution(mesh):
    placed = (
        P(("groups", "rows"), None, "proj"),
        P(("groups", "rows", "proj"), None),
        P(("groups", "rows"), None),
        P(("groups", "rows"), None, "proj"),
    )
    return jax.shard_map(
        functools.partial(on_device, mesh.shape["rows"]),
        mesh=mesh,
        in_specs=placed,
        out_specs=P(("groups", "rows"), "proj"),
        check_vma=False,
    )
```

time: 290 us -> 180 us (0.62)
  waiting for transfers between devices: 206 us -> 0 us
  Pallas kernels: 0 us -> 176 us
  matrix products: 61.2 us -> 0 us
  between operations: 13.4 us -> 0.01 us
    all_gather x1 -> x0, waiting for transfers between devices: 200 us -> none  [on_device(): lax.all_gather(queries, 'rows', axis=0, tiled=True)]
    pallas_call x0 -> x1, Pallas kernels: none -> 176 us  [on_device(): pl.pallas_call(functools.partial(kernel, n), out_shape=(jax.ShapeDtypeStr...]
    dot_general x2 -> x0, matrix products: 61.2 us -> none  [the longest x1 34 us: score_fold(): lax.dot_general(stacked, flat_block, (((1,), (1,)), ((), ())), precision=...]
    reduce_scatter x1 -> x0, waiting for transfers between devices: 6.08 us -> none  [on_device(): scores = lax.psum_scatter(totals, 'proj', scatter_dimension=1, tiled=True)]
  transfers between devices with their start and end apart: 2 -> 0, of which waited for: 2 -> 0; matrix products, arithmetic and copies ran while one was open for 10% -> 0% of each run, Pallas kernels for 0% -> 0%
where the time goes in v1:
time: 180 us
  Pallas kernels  176 us (98%)
  local copies, waits for them, and re-layouts  2.86 us (2%)
    pallas_call x1, Pallas kernels, on_device(): pl.pallas_call(functools.partial(kernel, n), out_shape=(jax.ShapeDtypeStr...  176 us

profile of v1, /device:TPU:0, one launch (start us, length us, event | category | flops | bytes accessed | tf_op | source)
XLA Modules:
  0.0 180.2 jit_solution(14157371010511500025)
XLA Ops:
  0.0 0.8 copy.5
  0.8 1.4 copy.6.weights
  2.2 0.7 broadcast_in_dim.3
  2.9 175.7 %shard_map.46 = (f32[8,32,4,4096]{3,2,1,0:T(4,128)}, f32[320,128]{1,0:T(8,128)}, f32[320,128]{1,0:T(8,128)}) custom-call(f32[320,4,4096]{2,1,0:T(4,128)} %train.1, f32[160,4]{1,0:T(8,128)} %copy.6.weights, s32[320,4]{1,0:T(8,128)} %bitcast.1, f32[32,4,4096]{2,1,0:T(4,128)} %queries.1), custom_call_target="tpu_custom_call" | custom-call | flops 32212254720 | bytes 20971520 | tf_op jit(solution)/shard_map/pallas_call | solution.py:273
  178.5 1.7 add_multiply_fusion

commit v2 on v1

--- a/solution.py
+++ b/solution.py
@@ -8,16 +8,17 @@
 from jax.sharding import PartitionSpec as P
 
 MESH = pl.DeviceIdType.MESH
-PIECES = 8
-LAG = 2
+PIECES = 16
+LAG = 3
 
 
 def kernel(n, train, weights, ckpt, queries, gat, mine, theirs,
-           th, tl, tbuf, qtile, acc, wfull, pout,
+           th, tl, tbuf, qtile, acc, wfull, tot,
            recv, send, fetch, tsem, wsem, psem):
     line = n // 2
-    main = PIECES - 1
-    per_step = main + 2
+    early = max(1, (PIECES - LAG - 1) // (2 * max(1, line - 2)))
+    main = PIECES - early
+    per_step = PIECES + early
     y_slots = PIECES + (line - 1) * main
     z_slots = (line - 1) * per_step
     slots = max(y_slots, z_slots)
@@ -50,14 +51,14 @@
         v = jnp.maximum(t - PIECES, 0)
         other = by_arrival(lax.div(v, main))
         zb = jnp.where(first, z, other)
-        piece = jnp.where(first, lax.rem(t + PIECES - 1, PIECES), lax.rem(v, main))
+        piece = jnp.where(first, lax.rem(t + main, PIECES), lax.rem(v, main))
         return zb * 2 + col, piece
 
     def z_item(t, start, sign):
         s, i = lax.div(t, per_step), lax.rem(t, per_step)
         zb = start + sign * s
-        col = jnp.where(i == per_step - 1, 1 - y, y)
-        piece = jnp.minimum(i, PIECES - 1)
+        col = jnp.where(i >= PIECES, 1 - y, y)
+        piece = jnp.where(i >= PIECES, i - early, i)
         ok = (t < z_slots) & (zb >= 0) & (zb < line)
         own = (s == 0) & (i < PIECES)
         return jnp.clip(zb, 0, line - 1) * 2 + col, piece, ok, own
@@ -112,7 +113,7 @@
         for start, sign in ((z - 1, -1), (z + 1, 1)):
             block, piece, ok, _ = z_item(t, start, sign)
             found.append((block, piece, ok))
-        found.append((me, lax.rem(t + PIECES - 1, PIECES), t < PIECES))
+        found.append((me, lax.rem(t + main, PIECES), t < PIECES))
         return found
 
     def fetch_copy(src, piece, t, j):
@@ -156,14 +157,14 @@
 
     def t_copy(u):
         return pltpu.make_async_copy(
-            part(train, lax.rem(u + PIECES - 1, PIECES)), tbuf.at[lax.rem(u, 2)], tsem.at[lax.rem(u, 2)])
+            part(train, lax.rem(u + main, PIECES)), tbuf.at[lax.rem(u, 2)], tsem.at[lax.rem(u, 2)])
 
     def split(u):
         @pl.when(u + 1 < PIECES)
         def _():
             t_copy(u + 1).start()
         t_copy(u).wait()
-        ds = pl.ds(pl.multiple_of(lax.rem(u + PIECES - 1, PIECES) * width, width), width)
+        ds = pl.ds(pl.multiple_of(lax.rem(u + main, PIECES) * width, width), width)
 
         def some(r, carry):
             x = tbuf[lax.rem(u, 2), pl.ds(r * 16, 16)].reshape(16 * ckpts, width)
@@ -195,6 +196,29 @@
         src_ref=weights, dst_ref=wfull.at[core], send_sem=wsem.at[0], recv_sem=wsem.at[1],
         device_id=partner, device_id_type=MESH)
 
+    def finish(zb):
+        half = lax.div(zb, line // 2)
+        first = (zb - half * (line // 2)) * 2 * count
+        w = jnp.concatenate([wfull[0], wfull[1]], axis=0)
+        held = ckpt[...]
+        of_lane = lax.broadcasted_iota(jnp.int32, (rows, lanes), 1) % ckpts
+        coef = [jnp.where(held[:, s:s + 1] == of_lane, w[:, s:s + 1], 0.0) for s in range(ckpts)]
+        both = []
+        for col in range(2):
+            a = acc.at[zb * 2 + col]
+            mixed = coef[0] * a[pl.ds(0, rows, stride=ckpts), :]
+            for s in range(1, ckpts):
+                mixed += coef[s] * a[pl.ds(s, rows, stride=ckpts), :]
+            both.append(mixed)
+        lane = lax.broadcasted_iota(jnp.int32, (2 * lanes, half_cols), 0)
+        col = lax.broadcasted_iota(jnp.int32, (2 * lanes, half_cols), 1)
+        place = jnp.where(col - first == lane // ckpts, 1.0, 0.0).astype(jnp.float32)
+        tot[half] += lax.dot_general(
+            jnp.concatenate(both, axis=1), place, (((1,), (0,)), ((), ())),
+            precision=lax.Precision.HIGHEST, preferred_element_type=jnp.float32)
+
+    full_from = max(PIECES + main * (line - 2), per_step * (line - 2)) + LAG + 1
+
     def clear(b, carry):
         acc[b] = jnp.zeros(acc.shape[1:], jnp.float32)
         return carry
@@ -209,6 +233,7 @@
             w_copy.start()
             wfull[core] = weights[...]
             lax.fori_loop(0, n, clear, 0)
+            tot[...] = jnp.zeros(tot.shape, jnp.float32)
 
         @pl.when((u >= LAG) & (u < slots + LAG))
         def _():
@@ -222,41 +247,30 @@
         def _():
             multiply(u - LAG - 1)
 
-        wait_sends(u - 4)
+        e = u - full_from
+
+        @pl.when(e == 0)
+        def _():
+            w_copy.wait()
+
+        @pl.when((e >= 0) & (e < line - 1))
+        def _():
+            finish(jnp.where(e == 0, z, by_arrival(jnp.maximum(e - 1, 0))))
+
+        wait_sends(u - 5)
         return carry
 
     last = slots + LAG + 1
     lax.fori_loop(0, last, step, 0)
-    for u in range(last - 4, slots):
+    for u in range(last - 5, slots):
         wait_sends(u)
-    w_copy.wait()
-
-    w = jnp.concatenate([wfull[0], wfull[1]], axis=0)
-    held = ckpt[...]
-    of_lane = lax.broadcasted_iota(jnp.int32, (rows, lanes), 1) % ckpts
-    coef = [jnp.where(held[:, s:s + 1] == of_lane, w[:, s:s + 1], 0.0) for s in range(ckpts)]
-
-    def finish(half):
-        def one(b, total):
-            block = half * (n // 2) + b
-            a = acc.at[block]
-            mixed = coef[0] * a[pl.ds(0, rows, stride=ckpts), :]
-            for s in range(1, ckpts):
-                mixed += coef[s] * a[pl.ds(s, rows, stride=ckpts), :]
-            lane = lax.broadcasted_iota(jnp.int32, (lanes, half_cols), 0)
-            col = lax.broadcasted_iota(jnp.int32, (lanes, half_cols), 1)
-            place = jnp.where(col - b * count == lane // ckpts, 1.0, 0.0).astype(jnp.float32)
-            return total + lax.dot_general(mixed, place, (((1,), (0,)), ((), ())),
-                                           precision=lax.Precision.HIGHEST,
-                                           preferred_element_type=jnp.float32)
-        return lax.fori_loop(0, n // 2, one, jnp.zeros((rows, half_cols), jnp.float32))
-
-    pout[...] = finish(1 - core)
+    finish(by_arrival(line - 2))
+
     back = pltpu.make_async_remote_copy(
-        src_ref=pout, dst_ref=theirs, send_sem=psem.at[0], recv_sem=psem.at[1],
+        src_ref=tot.at[1 - core], dst_ref=theirs, send_sem=psem.at[0], recv_sem=psem.at[1],
         device_id=partner, device_id_type=MESH)
     back.start()
-    mine[...] = finish(core)
+    mine[...] = tot[core]
     back.wait()
 
 
@@ -282,7 +296,7 @@
             pltpu.VMEM((2, 4, count, ckpts, width), jnp.float32),
             pltpu.VMEM((n, rows * ckpts, lanes), jnp.float32),
             pltpu.VMEM((2, rows // 2, ckpts), jnp.float32),
-            pltpu.VMEM((rows, half_cols), jnp.float32),
+            pltpu.VMEM((2, rows, half_cols), jnp.float32),
             pltpu.SemaphoreType.DMA((n, PIECES)),
             pltpu.SemaphoreType.DMA((3, 8)),
             pltpu.SemaphoreType.DMA((2, 4)),

time: 180 us -> 177 us (0.983)
  Pallas kernels: 176 us -> 172 us
    pallas_call x1, Pallas kernels: 176 us -> 172 us  [on_device(): pl.pallas_call(functools.partial(kernel, n), out_shape=(jax.ShapeDtypeStr...]
where the time goes in v2:
time: 177 us
  Pallas kernels  172 us (97%)
  local copies, waits for them, and re-layouts  2.86 us (2%)
    pallas_call x1, Pallas kernels, on_device(): pl.pallas_call(functools.partial(kernel, n), out_shape=(jax.ShapeDtypeStr...  172 us

profile of v2, /device:TPU:0, one launch (start us, length us, event | category | flops | bytes accessed | tf_op | source)
XLA Modules:
  0.0 176.5 jit_solution(16851441763893049893)
XLA Ops:
  0.0 0.8 copy.5
  0.8 1.4 copy.6.weights
  2.2 0.7 broadcast_in_dim.3
  2.9 172.0 %shard_map.46 = (f32[8,32,4,4096]{3,2,1,0:T(4,128)}, f32[320,128]{1,0:T(8,128)}, f32[320,128]{1,0:T(8,128)}) custom-call(f32[320,4,4096]{2,1,0:T(4,128)} %train.1, f32[160,4]{1,0:T(8,128)} %copy.6.weights, s32[320,4]{1,0:T(8,128)} %bitcast.1, f32[32,4,4096]{2,1,0:T(4,128)} %queries.1), custom_call_target="tpu_custom_call" | custom-call | flops 32212254720 | bytes 20971520 | tf_op jit(solution)/shard_map/pallas_call | solution.py:287
  174.8 1.7 add_multiply_fusion

commit v3 on v2

--- a/solution.py
+++ b/solution.py
@@ -13,7 +13,7 @@
 
 
 def kernel(n, train, weights, ckpt, queries, gat, mine, theirs,
-           th, tl, tbuf, qtile, acc, wfull, tot,
+           th, tl, tbuf, qtile, acc, wfull, wcol, hcol, tot,
            recv, send, fetch, tsem, wsem, psem):
     line = n // 2
     early = max(1, (PIECES - LAG - 1) // (2 * max(1, line - 2)))
@@ -191,7 +191,6 @@
 
     pl.semaphore_wait(barrier, 2 + (z < line - 1).astype(jnp.int32) + (z > 0).astype(jnp.int32))
 
-    here = weights.shape[0]
     w_copy = pltpu.make_async_remote_copy(
         src_ref=weights, dst_ref=wfull.at[core], send_sem=wsem.at[0], recv_sem=wsem.at[1],
         device_id=partner, device_id_type=MESH)
@@ -199,9 +198,8 @@
     def finish(zb):
         half = lax.div(zb, line // 2)
         first = (zb - half * (line // 2)) * 2 * count
-        w = jnp.concatenate([wfull[0], wfull[1]], axis=0)
-        held = ckpt[...]
-        of_lane = lax.broadcasted_iota(jnp.int32, (rows, lanes), 1) % ckpts
+        w, held = wcol[...], hcol[...]
+        of_lane = (lax.broadcasted_iota(jnp.int32, (rows, lanes), 1) % ckpts).astype(jnp.float32)
         coef = [jnp.where(held[:, s:s + 1] == of_lane, w[:, s:s + 1], 0.0) for s in range(ckpts)]
         both = []
         for col in range(2):
@@ -252,6 +250,13 @@
         @pl.when(e == 0)
         def _():
             w_copy.wait()
+            for c in range(2):
+                wcol[pl.ds(c * (rows // 2), rows // 2)] = wfull[c].T
+            slabs = ckpt.shape[1]
+            slab = lax.broadcasted_iota(jnp.int32, (slabs, rows), 0)
+            row = lax.broadcasted_iota(jnp.int32, (slabs, rows), 1)
+            spread = jnp.where(row // (rows // slabs) == slab, 1.0, 0.0).astype(jnp.float32)
+            hcol[...] = jnp.dot(ckpt[...].astype(jnp.float32), spread, preferred_element_type=jnp.float32).T
 
         @pl.when((e >= 0) & (e < line - 1))
         def _():
@@ -280,7 +285,6 @@
     lanes = count * ckpts
     width = depth // PIECES
     half_cols = n * count // 2
-    held = jnp.repeat(ckpt_index, rows // ckpt_index.shape[0], axis=0)
     anyspec = pl.BlockSpec(memory_space=pl.ANY)
     vmem = pl.BlockSpec(memory_space=pltpu.VMEM)
     part = jax.ShapeDtypeStruct((rows, half_cols), jnp.float32)
@@ -295,7 +299,9 @@
             pltpu.VMEM((2, rows, ckpts, width), jnp.float32),
             pltpu.VMEM((2, 4, count, ckpts, width), jnp.float32),
             pltpu.VMEM((n, rows * ckpts, lanes), jnp.float32),
-            pltpu.VMEM((2, rows // 2, ckpts), jnp.float32),
+            pltpu.VMEM((2, ckpts, rows // 2), jnp.float32),
+            pltpu.VMEM((rows, ckpts), jnp.float32),
+            pltpu.VMEM((rows, ckpts), jnp.float32),
             pltpu.VMEM((2, rows, half_cols), jnp.float32),
             pltpu.SemaphoreType.DMA((n, PIECES)),
             pltpu.SemaphoreType.DMA((3, 8)),
@@ -308,7 +314,7 @@
             collective_id=0, has_side_effects=True, vmem_limit_bytes=60 * 1024 * 1024),
         cost_estimate=pl.CostEstimate(
             flops=6 * rows * ckpts * depth * lanes * n, bytes_accessed=4 * rows * ckpts * depth, transcendentals=0),
-    )(train_rows, weights, held, queries)
+    )(train_rows, weights.T, ckpt_index.T, queries)
     return (mine + theirs) * (1.0 / ckpts)
 
 

time: 177 us -> 174 us (0.983)
  local copies, waits for them, and re-layouts: 2.86 us -> 0 us
    unnamed x2 -> x0, local copies, waits for them, and re-layouts: 2.19 us -> none
where the time goes in v3:
time: 174 us; the launch traced here: 173 us
  Pallas kernels  172 us (99%)
    pallas_call x1, Pallas kernels, on_device(): pl.pallas_call(functools.partial(kernel, n), out_shape=(jax.ShapeDtypeStr...  172 us

profile of v3, /device:TPU:0, one launch (start us, length us, event | category | flops | bytes accessed | tf_op | source)
XLA Modules:
  0.0 173.4 jit_solution(4596249014532537375)
XLA Ops:
  0.0 171.7 %shard_map.46 = (f32[8,32,4,4096]{3,2,1,0:T(4,128)}, f32[320,128]{1,0:T(8,128)}, f32[320,128]{1,0:T(8,128)}) custom-call(f32[320,4,4096]{2,1,0:T(4,128)} %train.1, f32[4,160]{1,0:T(4,128)} %bitcast.2, s32[4,20]{1,0:T(4,128)} %bitcast.3, f32[32,4,4096]{2,1,0:T(4,128)} %queries.1), custom_call_target="tpu_custom_call" | custom-call | flops 32212254720 | bytes 20971520 | tf_op jit(solution)/shard_map/pallas_call | solution.py:291
  171.7 1.7 add_multiply_fusion
